TPU v7x, 32 devices: a whole 2x2x4 slice. The times are simulated.
32 devices in a mesh: rows: 8 (over z, y), irrep: 4 (over x, core).
Axes of the slice: x: 2, y: 2, z: 4, core: 2. Of those that a mesh axis runs over, the one named last changes fastest.
Arguments:
- coefficients: float32 [4, 2560, 2560], P('irrep', 'rows'), may hold values from -6 to 6
- block_codes: int32 [4, 4, 4, 320], P('irrep'), may hold values from -1 to 19, as said below
- tile_bank: float32 [4, 4, 8, 128, 128], P('irrep'), may hold values from -0.125 to 0.125
Outputs:
- sigma_vector: float32 [4, 2560, 2560], P('irrep', 'rows')
Inputs may be any that keep to these rules, and one draw needn't show every extreme that they name: Fields 0 and 1 of block_codes[g, k] are block numbers below 20 for k = 0, 3 and below 20 for k = 1, 2; the first of them list the diagonal blocks 0, 1, ... in order, so every block row holds a listed block; field 2 is a tile number below 8; field 3 is -1 or +1.
All inputs are finite; a program needn't handle non-finite values.
Results may differ from a plain program's by a relative error of at most 0.0001.
Values sent between devices are 32-bit elements; how exact they have to be, the bound alone decides.
A program may use at most 256 MiB of HBM per device.

v0:
```python
import jax
import jax.numpy as jnp
from jax import lax
from jax.sharding import PartitionSpec as P

highest = lax.Precision.HIGHEST


def from_partner(shard, axis, bit):
    return lax.ppermute(shard, axis, [(i, i ^ 1 << bit) for i in range(lax.axis_size(axis))])


def apply_operator(values, block_codes, tile_bank):
    tile_size = tile_bank.shape[-1]
    tile_count = tile_bank.shape[0]
    block_count = values.shape[-1] // tile_size
    pieces = values.reshape(values.shape[0], block_count, tile_size)
    every_tile = jnp.einsum("rbq,tpq->rbtp", pieces, tile_bank, precision=highest)
    every_tile = every_tile.reshape(values.shape[0], block_count * tile_count, tile_size)
    flat_index = block_codes[1] * tile_count + block_codes[2]
    product = jnp.take(every_tile, flat_index, axis=1)
    placed = jnp.where(
        block_codes[0][:, None] == jnp.arange(block_count, dtype=jnp.int32)[None, :],
        block_codes[3][:, None].astype(jnp.float32),
        jnp.float32(0.0),
    )
    result = jnp.einsum("rkp,kb->rbp", product, placed, precision=highest)
    return result.reshape(values.shape[0], block_count * tile_size)


def applied(values, block_codes, tile_bank, which_op):
    return jax.vmap(apply_operator)(values, block_codes[:, which_op], tile_bank[:, which_op])


def body(coefficients, block_codes, tile_bank):
    flipped_bit = lax.axis_size("irrep").bit_length() - 2
    partner = from_partner(coefficients, "irrep", flipped_bit)
    beta_term = applied(coefficients, block_codes, tile_bank, 0)
    by_beta = jnp.swapaxes(coefficients, 1, 2)
    mixed = applied(partner, block_codes, tile_bank, 3)
    columns, cross_columns = (
        lax.all_to_all(by_beta, "rows", split_axis=1, concat_axis=2, tiled=True),
        lax.all_to_all(jnp.swapaxes(mixed, 1, 2), "rows", split_axis=1, concat_axis=2, tiled=True),
    )
    alpha_columns = applied(columns, block_codes, tile_bank, 1) + applied(
        cross_columns, block_codes, tile_bank, 2
    )
    returned = lax.all_to_all(alpha_columns, "rows", split_axis=2, concat_axis=1, tiled=True)
    sigma_vector = beta_term + jnp.swapaxes(returned, 1, 2)
    return sigma_vector


def solution(mesh):
    in_specs = (
        P("irrep", "rows", None),
        P("irrep", None, None, None),
        P("irrep", None, None, None, None),
    )
    out_specs = P("irrep", "rows", None)
    return jax.shard_map(body, mesh=mesh, in_specs=in_specs, out_specs=out_specs, check_vma=False)
```

profile of v0, /device:TPU:0, one launch (start us, length us, event | category | flops | bytes accessed | tf_op | source)
XLA Modules:
  0.0 786.8 jit_solution(13754017799785662038)
XLA Ops:
  0.0 2.9 collective-permute-start
  2.9 8.9 %copy.19 = f32[1,320,2560]{1,0,2:T(1,128)} copy(f32[1,320,2560]{2,1,0:T(8,128)} %param.5) | data formatting | bytes 6553600 | tf_op args[0]
  11.8 5.8 all-to-all-start
  17.6 4.6 reshape.595
  23.7 25.3 %fusion.14 = f32[320,20,8,128]{3,0,2,1:T(8,128)} fusion(f32[320,20,128,1]{2,1,0,3:T(8,128)} %bitcast.167, f32[1,4,8,128,128]{4,3,2,1,0:T(8,128)} %param.7), kind=kOutput, calls=%fused_computation.25 | convolution fusion | flops 10066329600 | bytes 30670848 | tf_op jit(solution)/shard_map/vmap(rbq,tpq->rbtp)/dot_general | solution.py:18
  48.9 40.0 %gather_fusion = f32[320,320,128]{2,1,0:T(8,128)} fusion(f32[1,320,160,128]{3,1,2,0:T(8,128)} %bitcast.160, s32[320]{0:T(512)S(1)} %fusion.74), kind=kCustom, calls=%fused_computation.clone | custom fusion | bytes 104860160 | tf_op jit(solution)/shard_map/vmap(jit(_take))/gather | solution.py:21
  93.5 25.3 %fusion.12 = f32[320,20,8,128]{3,0,2,1:T(8,128)} fusion(f32[320,20,128,1]{2,1,0,3:T(8,128)} %bitcast.168, f32[1,4,8,128,128]{4,3,2,1,0:T(8,128)} %param.7), kind=kOutput, calls=%fused_computation.23 | convolution fusion | flops 10066329600 | bytes 30670848 | tf_op jit(solution)/shard_map/vmap(rbq,tpq->rbtp)/dot_general | solution.py:18
  118.9 40.0 %gather_fusion.2 = f32[320,320,128]{2,1,0:T(8,128)} fusion(f32[1,320,160,128]{3,1,2,0:T(8,128)} %bitcast.161, s32[320]{0:T(512)S(1)} %fusion.76), kind=kCustom, calls=%fused_computation.2.clone | custom fusion | bytes 104860160 | tf_op jit(solution)/shard_map/vmap(jit(_take))/gather | solution.py:21
  158.9 35.0 %fusion.1 = f32[320,320,128]{2,0,1:T(8,128)} fusion(f32[320,320,128]{2,1,0:T(8,128)} %gather_fusion.2, pred[320]{0:T(512)(128)(4,1)S(1)} %get-tuple-element.18), kind=kLoop, calls=%fused_computation.7 | loop fusion | flops 13107200 | bytes 104857920 | tf_op jit(solution)/shard_map/reshape.44
  193.8 70.3 %fusion.19 = f32[1,320,20,128]{3,2,1,0:T(8,128)} fusion(f32[320,320,128]{2,0,1:T(8,128)} %fusion.1, f32[320]{0:T(512)S(1)} %get-tuple-element.22, s32[320]{0:T(512)S(1)} %get-tuple-element.24), kind=kOutput, calls=%fused_computation.28 | convolution fusion | flops 3145740800 | bytes 55708160 | tf_op jit(solution)/shard_map/vmap(rkp,kb->rbp)/dot_general | solution.py:27
  264.2 3.0 reshape.608
  267.2 6.1 copy.25
  273.3 6.0 all-to-all-start.1
  280.0 9.0 %copy.20 = f32[1,8,320,320]{2,3,1,0:T(8,128)} copy(f32[1,8,320,320]{3,0,2,1:T(1,128)} %bitcast.20) | data formatting | bytes 6553600 | tf_op jit(solution)/shard_map/all_to_all | solution.py:42
  289.0 29.7 %fusion.27 = f32[320,20,8,128]{3,0,2,1:T(8,128)} fusion(f32[320,20,128,1]{0,2,3,1:T(8,128)} %bitcast.164, f32[1,4,8,128,128]{4,3,2,1,0:T(8,128)} %param.7), kind=kOutput, calls=%fused_computation.32 | convolution fusion | flops 10066329600 | bytes 30670848 | tf_op jit(solution)/shard_map/vmap(rbq,tpq->rbtp)/dot_general | solution.py:18
  318.8 40.3 %gather_fusion.1 = f32[320,320,128]{2,1,0:T(8,128)} fusion(f32[1,320,160,128]{3,1,2,0:T(8,128)} %bitcast.162, s32[320]{0:T(512)S(1)} %fusion.75), kind=kCustom, calls=%fused_computation.1.clone | custom fusion | bytes 104860160 | tf_op jit(solution)/shard_map/vmap(jit(_take))/gather | solution.py:21
  359.1 35.0 %fusion.2 = f32[320,320,128]{2,0,1:T(8,128)} fusion(f32[320,320,128]{2,1,0:T(8,128)} %gather_fusion.1, pred[320]{0:T(512)(128)(4,1)S(1)} %copy-done.7), kind=kLoop, calls=%fused_computation.9 | loop fusion | flops 13107200 | bytes 104857920 | tf_op jit(solution)/shard_map/reshape.33
  394.1 9.0 %copy.26 = f32[1,8,320,320]{2,3,1,0:T(8,128)} copy(f32[1,8,320,320]{3,0,2,1:T(1,128)} %bitcast.52) | data formatting | bytes 6553600 | tf_op jit(solution)/shard_map/all_to_all | solution.py:43
  403.1 30.0 %fusion.24 = f32[320,20,8,128]{3,0,2,1:T(8,128)} fusion(f32[320,20,128,1]{0,2,3,1:T(8,128)} %bitcast.165, f32[1,4,8,128,128]{4,3,2,1,0:T(8,128)} %param.7), kind=kOutput, calls=%fused_computation.29 | convolution fusion | flops 10066329600 | bytes 30670848 | tf_op jit(solution)/shard_map/vmap(rbq,tpq->rbtp)/dot_general | solution.py:18
  433.1 40.3 %gather_fusion.3 = f32[320,320,128]{2,1,0:T(8,128)} fusion(f32[1,320,160,128]{3,1,2,0:T(8,128)} %bitcast.163, s32[320]{0:T(512)S(1)} %fusion.77), kind=kCustom, calls=%fused_computation.3.clone | custom fusion | bytes 104860160 | tf_op jit(solution)/shard_map/vmap(jit(_take))/gather | solution.py:21
  473.4 35.0 %fusion = f32[320,320,128]{2,0,1:T(8,128)} fusion(f32[320,320,128]{2,1,0:T(8,128)} %gather_fusion.3, pred[320]{0:T(512)(128)(4,1)S(1)} %copy-done.8), kind=kLoop, calls=%fused_computation.5 | loop fusion | flops 13107200 | bytes 104857920 | tf_op jit(solution)/shard_map/reshape.52
  508.4 69.3 %fusion.4 = f32[20,320,128]{2,0,1:T(8,128)S(1)} fusion(f32[320,320,128]{2,0,1:T(8,128)} %fusion, f32[320]{0:T(512)S(1)} %copy-done.2, s32[320]{0:T(512)S(1)} %copy-done.1), kind=kOutput, calls=%fused_computation.12 | convolution fusion | flops 3145740800 | bytes 55708160 | tf_op jit(solution)/shard_map/vmap(rkp,kb->rbp)/dot_general | solution.py:27
  577.7 70.2 %add_bitcast_fusion = f32[1,320,20,128]{3,2,1,0:T(8,128)} fusion(f32[20,320,128]{2,0,1:T(8,128)S(1)} %fusion.4, f32[320,320,128]{2,0,1:T(8,128)} %fusion.2, f32[320]{0:T(512)S(1)} %copy-done.5, s32[320]{0:T(512)S(1)} %copy-done.4), kind=kOutput, calls=%fused_computation.21 | convolution fusion | flops 3146560000 | bytes 58984960 | tf_op jit(solution)/shard_map/vmap(rkp,kb->rbp)/dot_general | solution.py:27
  647.9 3.0 add.96
  650.9 6.2 copy.29
  657.1 6.0 all-to-all-start.2
  663.1 35.0 %fusion.3 = f32[320,320,128]{2,0,1:T(8,128)} fusion(f32[320,320,128]{2,1,0:T(8,128)} %gather_fusion, pred[320]{0:T(512)(128)(4,1)S(1)} %copy-done.6), kind=kLoop, calls=%fused_computation.11 | loop fusion | flops 13107200 | bytes 104857920 | tf_op jit(solution)/shard_map/reshape.10
  698.2 69.9 %fusion.16 = f32[1,320,20,128]{3,2,1,0:T(8,128)} fusion(f32[320,320,128]{2,0,1:T(8,128)} %fusion.3, f32[320]{0:T(512)S(1)} %copy-done.3, s32[320]{0:T(512)S(1)} %copy-done), kind=kOutput, calls=%fused_computation.27 | convolution fusion | flops 3145740800 | bytes 55708160 | tf_op jit(solution)/shard_map/vmap(rkp,kb->rbp)/dot_general | solution.py:27
  768.2 3.0 reshape.599
  771.2 6.3 copy.62
  777.5 4.9 all_to_all.44
  782.3 4.1 bitcast_add_fusion
  (38 shorter events, 6.7 us)
Async XLA Ops:
  0.0 91.4 %collective-permute-start = (f32[1,320,2560]{2,1,0:T(8,128)}, f32[1,320,2560]{2,1,0:T(8,128)S(1)}, u32[]{:S(2)}, u32[]{:S(2)}) collective-permute-start(f32[1,320,2560]{2,1,0:T(8,128)} %param.5), channel_id=1, source_target_pairs={{0,2},{1,3},{2,0},{3,1},{4,6},{5,7},{6,4},{7,5},{8,10},{9,11},{10,... | collective-permute-start | bytes 9830408 | tf_op jit(solution)/shard_map/ppermute | solution.py:10
  11.8 261.5 %all-to-all-start = ((f32[1,2560,320]{2,0,1:T(1,128)}), f32[1,2560,320]{2,0,1:T(1,128)}, u32[]{:S(2)}, u32[]{:S(2)}) async-start(f32[1,2560,320]{2,0,1:T(1,128)} %bitcast.166), calls=%async_computation | async-start | bytes 7864320 | tf_op jit(solution)/shard_map/all_to_all | solution.py:42
  273.3 120.8 %all-to-all-start.1 = ((f32[1,2560,320]{2,0,1:T(1,128)}), f32[1,2560,320]{2,0,1:T(1,128)}, u32[]{:S(2)}, u32[]{:S(2)}) async-start(f32[1,2560,320]{2,0,1:T(1,128)} %copy.25), calls=%async_computation.1 | async-start | bytes 7864320 | tf_op jit(solution)/shard_map/all_to_all | solution.py:43
  318.8 40.3 %copy-start.7 = (pred[320]{0:T(512)(128)(4,1)S(1)}, pred[320]{0:T(512)(128)(4,1)}, u32[]{:S(2)}) copy-start(pred[320]{0:T(512)(128)(4,1)} %get-tuple-element.6) | copy-start | bytes 964
  433.1 40.3 %copy-start.8 = (pred[320]{0:T(512)(128)(4,1)S(1)}, pred[320]{0:T(512)(128)(4,1)}, u32[]{:S(2)}) copy-start(pred[320]{0:T(512)(128)(4,1)} %get-tuple-element.8) | copy-start | bytes 964
  473.4 35.0 %copy-start.1 = (s32[320]{0:T(512)S(1)}, s32[320]{0:T(512)}, u32[]{:S(2)}) copy-start(s32[320]{0:T(512)} %get-tuple-element.25) | copy-start | bytes 3844
  473.4 35.0 %copy-start.2 = (f32[320]{0:T(512)S(1)}, f32[320]{0:T(512)}, u32[]{:S(2)}) copy-start(f32[320]{0:T(512)} %get-tuple-element.23) | copy-start | bytes 3844
  508.4 69.3 %copy-start.4 = (s32[320]{0:T(512)S(1)}, s32[320]{0:T(512)}, u32[]{:S(2)}) copy-start(s32[320]{0:T(512)} %get-tuple-element.28) | copy-start | bytes 3844
  508.4 69.3 %copy-start.5 = (f32[320]{0:T(512)S(1)}, f32[320]{0:T(512)}, u32[]{:S(2)}) copy-start(f32[320]{0:T(512)} %get-tuple-element.26) | copy-start | bytes 3844
  577.7 85.4 %copy-start.6 = (pred[320]{0:T(512)(128)(4,1)S(1)}, pred[320]{0:T(512)(128)(4,1)}, u32[]{:S(2)}) copy-start(pred[320]{0:T(512)(128)(4,1)} %get-tuple-element.20) | copy-start | bytes 964
  657.1 114.1 %all-to-all-start.2 = ((f32[1,320,2560]{1,0,2:T(1,128)}), f32[1,320,2560]{1,0,2:T(1,128)}, u32[]{:S(2)}, u32[]{:S(2)}) async-start(f32[1,320,2560]{1,0,2:T(1,128)} %copy.29), calls=%async_computation.2 | async-start | bytes 7864320 | tf_op jit(solution)/shard_map/all_to_all | solution.py:48
  663.1 35.1 %copy-start = (s32[320]{0:T(512)S(1)}, s32[320]{0:T(512)}, u32[]{:S(2)}) copy-start(s32[320]{0:T(512)} %get-tuple-element.29) | copy-start | bytes 3844
  663.1 35.1 %copy-start.3 = (f32[320]{0:T(512)S(1)}, f32[320]{0:T(512)}, u32[]{:S(2)}) copy-start(f32[320]{0:T(512)} %get-tuple-element.27) | copy-start | bytes 3844
where the time goes:
time: 795 us; the launch traced here: 787 us
  matrix products  390 us (49%)
  local copies, waits for them, and re-layouts  229 us (29%)
  other arithmetic  147 us (18%)
  starting transfers between devices  20.8 us (3%)
    dot_general x4, matrix products, apply_operator(): result = jnp.einsum('rkp,kb->rbp', product, placed, precision=highest)  280 us
    gather x8, local copies, waits for them, and re-layouts, apply_operator(): product = jnp.take(every_tile, flat_index, axis=1)  161 us
    another operation x4, other arithmetic  140 us
    dot_general x4, matrix products, apply_operator(): jnp.einsum('rbq,tpq->rbtp', pieces, tile_bank, precision=highest)  110 us
  transfers between devices with their start and end apart: 4, of which 0 were waited for; matrix products, arithmetic and copies ran while one was open for 62% of the time, Pallas kernels for 0%

commit v1 on v0

v1 whole, which is shorter than its diff:
```python
import jax
import jax.numpy as jnp
from jax import lax
from jax.experimental import pallas as pl
from jax.experimental.pallas import tpu as pltpu
from jax.sharding import PartitionSpec as P

CONTRACT_LAST = (((1,), (1,)), ((), ()))


def from_partner(shard, axis, bit):
    return lax.ppermute(shard, axis, [(i, i ^ 1 << bit) for i in range(lax.axis_size(axis))])


def operator_kernel(codes, values, tiles, result, matrix, halves):
    rows, extent = values.shape
    tile_size = tiles.shape[-1]
    step = 2 * tile_size if extent % (2 * tile_size) == 0 else tile_size

    high = values[...].astype(jnp.bfloat16)
    halves[:rows, :] = high
    halves[rows:, :] = (values[...] - high.astype(jnp.float32)).astype(jnp.bfloat16)

    def clear(i, _):
        matrix[pl.ds(pl.multiple_of(i * tile_size, tile_size), tile_size), :] = jnp.zeros(
            (tile_size, extent), jnp.float32
        )
        return 0

    lax.fori_loop(0, extent // tile_size, clear, 0)

    def place(m, _):
        where = (
            pl.ds(pl.multiple_of(codes[0, m] * tile_size, tile_size), tile_size),
            pl.ds(pl.multiple_of(codes[1, m] * tile_size, tile_size), tile_size),
        )
        matrix[where] += codes[3, m].astype(jnp.float32) * tiles[codes[2, m]]
        return 0

    lax.fori_loop(0, codes.shape[1], place, 0)

    def multiply(i, _):
        part = pl.ds(pl.multiple_of(i * step, step), step)
        block = matrix[part, :]
        block_high = block.astype(jnp.bfloat16)
        block_low = (block - block_high.astype(jnp.float32)).astype(jnp.bfloat16)
        both = lax.dot_general(
            halves[...], block_high, CONTRACT_LAST, preferred_element_type=jnp.float32
        )
        rest = lax.dot_general(
            halves[:rows, :], block_low, CONTRACT_LAST, preferred_element_type=jnp.float32
        )
        result[:, part] = both[:rows] + (both[rows:] + rest)
        return 0

    lax.fori_loop(0, extent // step, multiply, 0)


def apply_operator(values, block_codes, tile_bank):
    rows, extent = values.shape
    vmem = pl.BlockSpec(memory_space=pltpu.VMEM)
    return pl.pallas_call(
        operator_kernel,
        out_shape=jax.ShapeDtypeStruct((rows, extent), jnp.float32),
        in_specs=[pl.BlockSpec(memory_space=pltpu.SMEM), vmem, vmem],
        out_specs=vmem,
        scratch_shapes=[
            pltpu.VMEM((extent, extent), jnp.float32),
            pltpu.VMEM((2 * rows, extent), jnp.bfloat16),
        ],
        compiler_params=pltpu.CompilerParams(vmem_limit_bytes=56 * 2**20),
        cost_estimate=pl.CostEstimate(
            flops=6 * rows * extent * extent, bytes_accessed=8 * rows * extent, transcendentals=0
        ),
    )(block_codes, values, tile_bank)


def applied(values, block_codes, tile_bank, which_op):
    return jnp.stack(
        [
            apply_operator(values[g], block_codes[g, which_op], tile_bank[g, which_op])
            for g in range(values.shape[0])
        ]
    )


def body(coefficients, block_codes, tile_bank):
    flipped_bit = lax.axis_size("irrep").bit_length() - 2
    partner = from_partner(coefficients, "irrep", flipped_bit)
    by_beta = jnp.swapaxes(coefficients, 1, 2)
    beta_term = applied(coefficients, block_codes, tile_bank, 0)
    columns = lax.all_to_all(by_beta, "rows", split_axis=1, concat_axis=2, tiled=True)
    mixed = applied(partner, block_codes, tile_bank, 3)
    cross_columns = lax.all_to_all(
        jnp.swapaxes(mixed, 1, 2), "rows", split_axis=1, concat_axis=2, tiled=True
    )
    alpha_columns = applied(columns, block_codes, tile_bank, 1) + applied(
        cross_columns, block_codes, tile_bank, 2
    )
    returned = lax.all_to_all(alpha_columns, "rows", split_axis=2, concat_axis=1, tiled=True)
    return beta_term + jnp.swapaxes(returned, 1, 2)


def solution(mesh):
    in_specs = (
        P("irrep", "rows", None),
        P("irrep", None, None, None),
        P("irrep", None, None, None, None),
    )
    out_specs = P("irrep", "rows", None)
    return jax.shard_map(body, mesh=mesh, in_specs=in_specs, out_specs=out_specs, check_vma=False)
```

time: 795 us -> 372 us (0.47)
  matrix products: 390 us -> 0 us
  waiting for transfers between devices: 0.01 us -> 175 us
  local copies, waits for them, and re-layouts: 229 us -> 61.1 us
  other arithmetic: 147 us -> 6.45 us
  Pallas kernels: 0 us -> 109 us
    dot_general x8 -> x0, matrix products: 390 us -> none  [the longest x4 280 us: apply_operator(): result = jnp.einsum('rkp,kb->rbp', product, placed, precision=highest)]
    gather x8 -> x0, local copies, waits for them, and re-layouts: 161 us -> none  [apply_operator(): product = jnp.take(every_tile, flat_index, axis=1)]
    another operation x4 -> x0, other arithmetic: 140 us -> none
    pallas_call x0 -> x4, Pallas kernels: none -> 109 us  [apply_operator(): pl.pallas_call(operator_kernel, out_shape=jax.ShapeDtypeStruct((rows, ext...]
    ppermute x1, waiting for transfers between devices: 0.01 us -> 67.4 us  [from_partner(): lax.ppermute(shard, axis, [(i, i ^ 1 << bit) for i in range(lax.axis_size...]
    all_to_all x1, waiting for transfers between devices: 0.01 us -> 59.6 us  [body(): lax.all_to_all(alpha_columns, 'rows', split_axis=2, concat_axis=1, tiled=...]
    all_to_all x1, waiting for transfers between devices: 0.01 us -> 47.8 us  [body(): lax.all_to_all(jnp.swapaxes(mixed, 1, 2), 'rows', split_axis=1, concat_ax...]
    squeeze x1 -> x4, local copies, waits for them, and re-layouts: 0.74 us -> 13.2 us  [the longest x2 9.7 us: applied(): values[g]]
  transfers between devices with their start and end apart: 4 -> 4, of which waited for: 0 -> 3; matrix products, arithmetic and copies ran while one was open for 62% -> 6% of each run, Pallas kernels for 0% -> 22%
where the time goes in v1:
time: 372 us; the launch traced here: 371 us
  waiting for transfers between devices  175 us (47%)
  Pallas kernels  109 us (29%)
  local copies, waits for them, and re-layouts  61.1 us (16%)
  starting transfers between devices  19.5 us (5%)
  other arithmetic  6.45 us (2%)
    pallas_call x4, Pallas kernels, apply_operator(): pl.pallas_call(operator_kernel, out_shape=jax.ShapeDtypeStruct((rows, ext...  109 us
    ppermute x1, waiting for transfers between devices, from_partner(): lax.ppermute(shard, axis, [(i, i ^ 1 << bit) for i in range(lax.axis_size...  67.4 us
    all_to_all x1, waiting for transfers between devices, body(): lax.all_to_all(alpha_columns, 'rows', split_axis=2, concat_axis=1, tiled=...  59.6 us
    all_to_all x1, waiting for transfers between devices, body(): lax.all_to_all(jnp.swapaxes(mixed, 1, 2), 'rows', split_axis=1, concat_ax...  47.8 us
    unnamed x9, local copies, waits for them, and re-layouts  10.6 us
    squeeze x2, local copies, waits for them, and re-layouts, applied(): values[g]  9.7 us
    all_to_all x2, local copies, waits for them, and re-layouts, body(): lax.all_to_all(alpha_columns, 'rows', split_axis=2, concat_axis=1, tiled=...  9.52 us
    transpose x1, local copies, waits for them, and re-layouts, body(): jnp.swapaxes(mixed, 1, 2)  8.99 us
  transfers between devices with their start and end apart: 4, of which 3 were waited for; matrix products, arithmetic and copies ran while one was open for 6% of the time, Pallas kernels for 22%

profile of v1, /device:TPU:0, one launch (start us, length us, event | category | flops | bytes accessed | tf_op | source)
XLA Modules:
  0.0 371.1 jit_solution(3162821323306232587)
XLA Ops:
  0.0 8.9 %copy.7 = f32[1,320,2560]{1,0,2:T(1,128)} copy(f32[1,320,2560]{2,1,0:T(8,128)} %param.3) | data formatting | bytes 6553600 | tf_op args[0]
  8.9 0.0 copy-start
  8.9 0.0 copy-start.2
  8.9 7.5 %all-to-all-start = ((f32[1,2560,320]{2,0,1:T(1,128)}), f32[1,2560,320]{2,0,1:T(1,128)}, u32[]{:S(2)}, u32[]{:S(2)}) async-start(f32[1,2560,320]{2,0,1:T(1,128)} %bitcast.48), calls=%async_computation | async-start | bytes 7864320 | tf_op jit(solution)/shard_map/all_to_all | solution.py:92
  16.5 0.0 copy-done
  16.5 1.6 collective-permute-start
  18.0 0.0 copy-done.2
  18.0 0.6 slice_bitcast_fusion.7
  18.6 2.9 slice_bitcast_fusion.3
  21.5 67.4 %collective-permute-done = f32[1,320,2560]{2,1,0:T(8,128)S(1)} collective-permute-done((f32[1,320,2560]{2,1,0:T(8,128)S(1)}, f32[1,320,2560]{2,1,0:T(8,128)S(1)}, u32[]{:S(2)}, u32[]{:S(2)}) %collective-permute-start) | collective-permute-done | bytes 3276832 | tf_op jit(solution)/shard_map/ppermute | solution.py:12
  88.9 0.0 copy-start.3
  88.9 1.7 copy-done.3
  90.6 27.3 %shard_map.39 = f32[320,2560]{1,0:T(8,128)} custom-call(s32[4,320]{1,0:T(4,128)} %get-tuple-element.11.codes, f32[320,2560]{1,0:T(8,128)} %bitcast.54, f32[8,128,128]{2,1,0:T(8,128)} %get-tuple-element.8.tiles), custom_call_target="tpu_custom_call" | custom-call | flops 12582912000 | bytes 6553600 | tf_op jit(solution)/shard_map/pallas_call | solution.py:62
  117.9 9.0 %copy.9 = f32[1,2560,320]{2,0,1:T(1,128)} copy(f32[1,2560,320]{1,2,0:T(8,128)} %bitcast.53) | data formatting | bytes 6553600 | tf_op jit(solution)/shard_map/transpose | solution.py:95
  126.9 0.0 all-to-all-done
  126.9 5.7 %all-to-all-start.1 = ((f32[1,2560,320]{2,0,1:T(1,128)}), f32[1,2560,320]{2,0,1:T(1,128)}, u32[]{:S(2)}, u32[]{:S(2)}) async-start(f32[1,2560,320]{2,0,1:T(1,128)} %copy.9), calls=%async_computation.1 | async-start | bytes 7864320 | tf_op jit(solution)/shard_map/all_to_all | solution.py:94
  132.6 6.3 %copy.18 = f32[1,8,320,320]{3,1,2,0:T(8,128)} copy(f32[1,8,320,320]{3,0,2,1:T(1,128)} %bitcast.6) | data formatting | bytes 6553600 | tf_op jit(solution)/shard_map/all_to_all | solution.py:92
  138.9 4.9 %squeeze.40.values = f32[320,2560]{1,0:T(8,128)} reshape(f32[1,320,8,320]{3,2,1,0:T(8,128)} %bitcast.49) | data formatting | bytes 6553600 | tf_op jit(solution)/shard_map/squeeze | solution.py:81
  143.7 27.3 %shard_map.38 = f32[320,2560]{1,0:T(8,128)} custom-call(s32[4,320]{1,0:T(4,128)} %get-tuple-element.10.codes, f32[320,2560]{1,0:T(8,128)} %squeeze.40.values, f32[8,128,128]{2,1,0:T(8,128)} %get-tuple-element.6.tiles), custom_call_target="tpu_custom_call" | custom-call | flops 12582912000 | bytes 6553600 | tf_op jit(solution)/shard_map/pallas_call | solution.py:62
  171.0 47.8 %all-to-all-done.1 = f32[1,2560,320]{2,0,1:T(1,128)} async-done(((f32[1,2560,320]{2,0,1:T(1,128)}), f32[1,2560,320]{2,0,1:T(1,128)}, u32[]{:S(2)}, u32[]{:S(2)}) %all-to-all-start.1) | async-done | bytes 3276832 | tf_op jit(solution)/shard_map/all_to_all | solution.py:94
  218.8 6.3 %copy.17 = f32[1,8,320,320]{3,1,2,0:T(8,128)} copy(f32[1,8,320,320]{3,0,2,1:T(1,128)} %bitcast.15) | data formatting | bytes 6553600 | tf_op jit(solution)/shard_map/all_to_all | solution.py:94
  225.1 4.9 %squeeze.46.values = f32[320,2560]{1,0:T(8,128)} reshape(f32[1,320,8,320]{3,2,1,0:T(8,128)} %bitcast.50) | data formatting | bytes 6553600 | tf_op jit(solution)/shard_map/squeeze | solution.py:81
  230.0 27.4 %shard_map.40 = f32[320,2560]{1,0:T(8,128)} custom-call(s32[4,320]{1,0:T(4,128)} %get-tuple-element.12.codes, f32[320,2560]{1,0:T(8,128)} %squeeze.46.values, f32[8,128,128]{2,1,0:T(8,128)} %get-tuple-element.7.tiles), custom_call_target="tpu_custom_call" | custom-call | flops 12582912000 | bytes 6553600 | tf_op jit(solution)/shard_map/pallas_call | solution.py:62
  257.4 0.0 copy-done.1
  257.4 2.4 add_bitcast_fusion
  259.7 6.2 %copy.11 = f32[1,320,2560]{1,0,2:T(1,128)} copy(f32[1,320,2560]{2,1,0:T(8,128)S(1)} %add_bitcast_fusion) | data formatting | bytes 6553600 | tf_op jit(solution)/shard_map/add | solution.py:97
  265.9 4.7 %all-to-all-start.2 = ((f32[1,320,2560]{1,0,2:T(1,128)}), f32[1,320,2560]{1,0,2:T(1,128)}, u32[]{:S(2)}, u32[]{:S(2)}) async-start(f32[1,320,2560]{1,0,2:T(1,128)} %copy.11), calls=%async_computation.2 | async-start | bytes 7864320 | tf_op jit(solution)/shard_map/all_to_all | solution.py:100
  270.7 27.3 %shard_map.37 = f32[320,2560]{1,0:T(8,128)} custom-call(s32[4,320]{1,0:T(4,128)} %get-tuple-element.9.codes, f32[320,2560]{1,0:T(8,128)} %bitcast.52, f32[8,128,128]{2,1,0:T(8,128)} %get-tuple-element.5.tiles), custom_call_target="tpu_custom_call" | custom-call | flops 12582912000 | bytes 6553600 | tf_op jit(solution)/shard_map/pallas_call | solution.py:62
  298.0 59.6 %all-to-all-done.2 = f32[1,320,2560]{1,0,2:T(1,128)} async-done(((f32[1,320,2560]{1,0,2:T(1,128)}), f32[1,320,2560]{1,0,2:T(1,128)}, u32[]{:S(2)}, u32[]{:S(2)}) %all-to-all-start.2) | async-done | bytes 3276832 | tf_op jit(solution)/shard_map/all_to_all | solution.py:100
  357.5 6.3 %copy.16 = f32[1,320,8,320]{1,2,3,0:T(8,128)} copy(f32[1,320,8,320]{1,0,3,2:T(1,128)} %bitcast.19) | data formatting | bytes 6553600 | tf_op jit(solution)/shard_map/all_to_all | solution.py:100
  363.8 3.2 all_to_all.44
  367.1 4.1 %bitcast_add_fusion = f32[1,320,2560]{2,1,0:T(8,128)} fusion(f32[1,2560,320]{1,2,0:T(8,128)S(1)} %all_to_all.44, f32[320,2560]{1,0:T(8,128)} %shard_map.37), kind=kLoop, calls=%fused_computation.3 | loop fusion | flops 819200 | bytes 9830400 | tf_op jit(solution)/shard_map/add | solution.py:101
  (1 shorter events, 0.0 us)
Async XLA Ops:
  8.9 7.6 %copy-start = (f32[1,320,2560]{2,1,0:T(8,128)S(1)}, f32[1,320,2560]{2,1,0:T(8,128)}, u32[]{:S(2)}) copy-start(f32[1,320,2560]{2,1,0:T(8,128)} %param.3) | copy-start | bytes 9830404
  8.9 9.1 %copy-start.2 = (s32[1,4,4,320]{3,2,1,0:T(4,128)S(1)}, s32[1,4,4,320]{3,2,1,0:T(4,128)}, u32[]{:S(2)}) copy-start(s32[1,4,4,320]{3,2,1,0:T(4,128)} %param.4) | copy-start | bytes 61444
  8.9 118.0 %all-to-all-start = ((f32[1,2560,320]{2,0,1:T(1,128)}), f32[1,2560,320]{2,0,1:T(1,128)}, u32[]{:S(2)}, u32[]{:S(2)}) async-start(f32[1,2560,320]{2,0,1:T(1,128)} %bitcast.48), calls=%async_computation | async-start | bytes 7864320 | tf_op jit(solution)/shard_map/all_to_all | solution.py:92
  16.5 72.4 %collective-permute-start = (f32[1,320,2560]{2,1,0:T(8,128)S(1)}, f32[1,320,2560]{2,1,0:T(8,128)S(1)}, u32[]{:S(2)}, u32[]{:S(2)}) collective-permute-start(f32[1,320,2560]{2,1,0:T(8,128)S(1)} %copy-done), channel_id=1, source_target_pairs={{0,2},{1,3},{2,0},{3,1},{4,6},{5,7},{6,4},{7,5},{8,10},{9,11},{10,... | collective-permute-start | bytes 9830408 | tf_op jit(solution)/shard_map/ppermute | solution.py:12
  88.9 1.7 copy-start.3
  126.9 91.9 %all-to-all-start.1 = ((f32[1,2560,320]{2,0,1:T(1,128)}), f32[1,2560,320]{2,0,1:T(1,128)}, u32[]{:S(2)}, u32[]{:S(2)}) async-start(f32[1,2560,320]{2,0,1:T(1,128)} %copy.9), calls=%async_computation.1 | async-start | bytes 7864320 | tf_op jit(solution)/shard_map/all_to_all | solution.py:94
  229.9 27.4 %copy-start.1 = (f32[320,2560]{1,0:T(8,128)S(1)}, f32[320,2560]{1,0:T(8,128)}, u32[]{:S(2)}) copy-start(f32[320,2560]{1,0:T(8,128)} %shard_map.38) | copy-start | bytes 9830404
  265.9 91.6 %all-to-all-start.2 = ((f32[1,320,2560]{1,0,2:T(1,128)}), f32[1,320,2560]{1,0,2:T(1,128)}, u32[]{:S(2)}, u32[]{:S(2)}) async-start(f32[1,320,2560]{1,0,2:T(1,128)} %copy.11), calls=%async_computation.2 | async-start | bytes 7864320 | tf_op jit(solution)/shard_map/all_to_all | solution.py:100

commit v2 on v1

--- a/solution.py
+++ b/solution.py
@@ -12,7 +12,8 @@
     return lax.ppermute(shard, axis, [(i, i ^ 1 << bit) for i in range(lax.axis_size(axis))])
 
 
-def operator_kernel(codes, values, tiles, result, matrix, halves):
+def operator_kernel(codes, values, tiles, *refs):
+    *base, result, matrix, halves = refs
     rows, extent = values.shape
     tile_size = tiles.shape[-1]
     step = 2 * tile_size if extent % (2 * tile_size) == 0 else tile_size
@@ -50,19 +51,20 @@
         rest = lax.dot_general(
             halves[:rows, :], block_low, CONTRACT_LAST, preferred_element_type=jnp.float32
         )
-        result[:, part] = both[:rows] + (both[rows:] + rest)
+        product = both[:rows] + (both[rows:] + rest)
+        result[:, part] = base[0][:, part] + product if base else product
         return 0
 
     lax.fori_loop(0, extent // step, multiply, 0)
 
 
-def apply_operator(values, block_codes, tile_bank):
+def apply_operator(values, block_codes, tile_bank, *base):
     rows, extent = values.shape
     vmem = pl.BlockSpec(memory_space=pltpu.VMEM)
     return pl.pallas_call(
         operator_kernel,
         out_shape=jax.ShapeDtypeStruct((rows, extent), jnp.float32),
-        in_specs=[pl.BlockSpec(memory_space=pltpu.SMEM), vmem, vmem],
+        in_specs=[pl.BlockSpec(memory_space=pltpu.SMEM)] + [vmem] * (2 + len(base)),
         out_specs=vmem,
         scratch_shapes=[
             pltpu.VMEM((extent, extent), jnp.float32),
@@ -72,33 +74,110 @@
         cost_estimate=pl.CostEstimate(
             flops=6 * rows * extent * extent, bytes_accessed=8 * rows * extent, transcendentals=0
         ),
-    )(block_codes, values, tile_bank)
+    )(block_codes, values, tile_bank, *base)
 
 
-def applied(values, block_codes, tile_bank, which_op):
-    return jnp.stack(
-        [
-            apply_operator(values[g], block_codes[g, which_op], tile_bank[g, which_op])
-            for g in range(values.shape[0])
-        ]
+def column_plan(extent, count, rows, tile_size):
+    parts = extent // (count * tile_size)
+    rest = extent // count - parts * tile_size
+    if parts and rest == 0:
+        return parts, tile_size, 0
+    narrow = rest // max(parts, 1)
+    if parts and rest % parts == 0 and tile_size % narrow == 0 and rows % (8 * tile_size // narrow) == 0:
+        return parts, tile_size, narrow
+    return 1, 0, extent // count
+
+
+def fold(blocks, width):
+    count, rows, narrow = blocks.shape
+    times = width // narrow
+    folded = blocks.reshape(count, times, rows // times, narrow)
+    return jnp.swapaxes(folded, 1, 2).reshape(count, rows // times, width)
+
+
+def unfold(packed, narrow):
+    count, rows, width = packed.shape
+    folded = packed.reshape(count, rows, width // narrow, narrow)
+    return jnp.swapaxes(folded, 1, 2).reshape(count, rows * (width // narrow), narrow)
+
+
+def exchange(packed):
+    return lax.all_to_all(packed, "rows", split_axis=0, concat_axis=0, tiled=True)
+
+
+def one_irrep(own, codes, bank, partner_codes, partner_tiles, bit):
+    count = lax.axis_size("rows")
+    rows, extent = own.shape
+    parts, wide, narrow = column_plan(extent, count, rows, bank.shape[-1])
+    width = wide + narrow
+
+    def join(whole, rest):
+        pieces = [whole] if wide else []
+        if narrow:
+            pieces.append(fold(rest, wide or narrow))
+        return jnp.concatenate(pieces, axis=1)
+
+    def split(packed):
+        rest = unfold(packed[:, rows if wide else 0 :], narrow) if narrow else None
+        return packed[:, :rows] if wide else None, rest
+
+    def outgoing(values, part):
+        def blocks(start, size):
+            start += part * count * size
+            return jnp.swapaxes(values[:, start : start + count * size].reshape(rows, count, size), 0, 1)
+
+        return join(blocks(0, wide), blocks(parts * count * wide, narrow))
+
+    def by_beta(arrived):
+        blocks = [x for x in split(arrived) if x is not None]
+        return jnp.concatenate([x.reshape(count * rows, x.shape[-1]).T for x in blocks], axis=0)
+
+    def by_alpha(columns):
+        return join(
+            columns[:wide].T.reshape(count, rows, wide), columns[wide:].T.reshape(count, rows, narrow)
+        )
+
+    def home(blocks):
+        return jnp.swapaxes(blocks, 0, 1).reshape(rows, count * blocks.shape[-1])
+
+    packed, own = lax.optimization_barrier(
+        (jnp.concatenate([outgoing(own, p) for p in range(parts)], axis=1), own)
     )
+    sent = exchange(packed)
+    length = sent.shape[1] // parts
+    mixed = apply_operator(own, partner_codes, partner_tiles)
+    crossing = [from_partner(outgoing(mixed, p), "irrep", bit) for p in range(parts)]
+    sent, crossing[0] = lax.optimization_barrier((sent, crossing[0]))
+    columns = jnp.concatenate(
+        [by_beta(sent[:, p * length : (p + 1) * length]) for p in range(parts)], axis=0
+    )
+    beta_term = apply_operator(own, codes[0], bank[0])
+    alpha_own = apply_operator(columns, codes[1], bank[1])
+    crossed = [exchange(x) for x in crossing]
+    returned = []
+    for p in range(parts):
+        total = by_alpha(
+            apply_operator(by_beta(crossed[p]), codes[2], bank[2], alpha_own[p * width : (p + 1) * width])
+        )
+        if p + 1 < parts:
+            crossed[p + 1], total = lax.optimization_barrier((crossed[p + 1], total))
+        returned.append(split(exchange(total)))
+    pieces = [home(x[k]) for k in range(2) for x in returned if x[k] is not None]
+    return beta_term + jnp.concatenate(pieces, axis=1)
 
 
 def body(coefficients, block_codes, tile_bank):
-    flipped_bit = lax.axis_size("irrep").bit_length() - 2
-    partner = from_partner(coefficients, "irrep", flipped_bit)
-    by_beta = jnp.swapaxes(coefficients, 1, 2)
-    beta_term = applied(coefficients, block_codes, tile_bank, 0)
-    columns = lax.all_to_all(by_beta, "rows", split_axis=1, concat_axis=2, tiled=True)
-    mixed = applied(partner, block_codes, tile_bank, 3)
-    cross_columns = lax.all_to_all(
-        jnp.swapaxes(mixed, 1, 2), "rows", split_axis=1, concat_axis=2, tiled=True
+    bit = lax.axis_size("irrep").bit_length() - 2
+    partner_tiles = from_partner(tile_bank[:, 3], "irrep", bit)
+    partner_codes = from_partner(block_codes[:, 3], "irrep", bit)
+    return jnp.stack(
+        [
+            one_irrep(
+                coefficients[g], block_codes[g], tile_bank[g], partner_codes[g], partner_tiles[g], bit
+            )
+            for g in range(coefficients.shape[0])
+        ]
     )
-    alpha_columns = applied(columns, block_codes, tile_bank, 1) + applied(
-        cross_columns, block_codes, tile_bank, 2
-    )
-    returned = lax.all_to_all(alpha_columns, "rows", split_axis=2, concat_axis=1, tiled=True)
-    return beta_term + jnp.swapaxes(returned, 1, 2)
 
 
 def solution(mesh):

time: 372 us -> 334 us (0.90)
  waiting for transfers between devices: 175 us -> 45.9 us
  local copies, waits for them, and re-layouts: 61.1 us -> 111 us
  starting transfers between devices: 19.5 us -> 35.8 us
  Pallas kernels: 109 us -> 125 us
  other arithmetic: 6.45 us -> 14 us
    all_to_all x3 -> x5, waiting for transfers between devices: 107 us -> 0.01 us  [exchange(): lax.all_to_all(packed, 'rows', split_axis=0, concat_axis=0, tiled=True)]
    reshape x0 -> x26, local copies, waits for them, and re-layouts: none -> 37.6 us  [the longest x8 10.5 us: fold(): folded = blocks.reshape(count, times, rows // times, narrow)]
    slice x0 -> x22, local copies, waits for them, and re-layouts: none -> 29 us  [the longest x12 10.7 us: split(): rest = unfold(packed[:, rows if wide else 0:], narrow) if narrow else None]
    all_to_all x4 -> x0, local copies, waits for them, and re-layouts: 22.1 us -> none  [the longest x2 9.52 us: body(): lax.all_to_all(alpha_columns, 'rows', split_axis=2, concat_axis=1, tiled=...]
    ppermute x1 -> x4, waiting for transfers between devices: 67.4 us -> 45.9 us  [from_partner(): lax.ppermute(shard, axis, [(i, i ^ 1 << bit) for i in range(lax.axis_size...]
    pallas_call x4 -> x5, Pallas kernels: 109 us -> 125 us  [apply_operator(): pl.pallas_call(operator_kernel, out_shape=jax.ShapeDtypeStruct((rows, ext...]
    all_to_all x3 -> x5, starting transfers between devices: 18 us -> 30.7 us  [exchange(): lax.all_to_all(packed, 'rows', split_axis=0, concat_axis=0, tiled=True)]
    transpose x1 -> x13, local copies, waits for them, and re-layouts: 8.99 us -> 21.5 us  [the longest x6 10.2 us: unfold(): jnp.swapaxes(folded, 1, 2).reshape(count, rows * (width // narrow), narrow)]
  transfers between devices with their start and end apart: 4 -> 9, of which waited for: 3 -> 2; matrix products, arithmetic and copies ran while one was open for 6% -> 29% of each run, Pallas kernels for 22% -> 38%
where the time goes in v2:
time: 334 us; the launch traced here: 332 us
  Pallas kernels  125 us (37%)
  local copies, waits for them, and re-layouts  111 us (33%)
  waiting for transfers between devices  45.9 us (14%)
  starting transfers between devices  35.8 us (11%)
  other arithmetic  14 us (4%)
    pallas_call x5, Pallas kernels, apply_operator(): pl.pallas_call(operator_kernel, out_shape=jax.ShapeDtypeStruct((rows, ext...  125 us
    ppermute x4, waiting for transfers between devices, from_partner(): lax.ppermute(shard, axis, [(i, i ^ 1 << bit) for i in range(lax.axis_size...  45.9 us
    all_to_all x5, starting transfers between devices, exchange(): lax.all_to_all(packed, 'rows', split_axis=0, concat_axis=0, tiled=True)  30.7 us
    slice x12, local copies, waits for them, and re-layouts, split(): rest = unfold(packed[:, rows if wide else 0:], narrow) if narrow else None  10.7 us
    reshape x8, local copies, waits for them, and re-layouts, fold(): folded = blocks.reshape(count, times, rows // times, narrow)  10.5 us
    transpose x6, local copies, waits for them, and re-layouts, unfold(): jnp.swapaxes(folded, 1, 2).reshape(count, rows * (width // narrow), narrow)  10.2 us
    reshape x6, local copies, waits for them, and re-layouts, fold(): return jnp.swapaxes(folded, 1, 2).reshape(count, rows // times, width)  9.53 us
    slice x6, local copies, waits for them, and re-layouts, blocks(): values[:, start:start + count * size].reshape(rows, count, size)  8.94 us
  transfers between devices with their start and end apart: 9, of which 2 were waited for; matrix products, arithmetic and copies ran while one was open for 29% of the time, Pallas kernels for 38%

profile of v2, /device:TPU:0, one launch (start us, length us, event | category | flops | bytes accessed | tf_op | source)
XLA Modules:
  0.0 331.8 jit_solution(3953476373013974220)
XLA Ops:
  13.5 7.3 %all-to-all-start.1 = ((f32[8,800,128]{2,1,0:T(8,128)}), f32[8,800,128]{2,1,0:T(8,128)S(1)}, u32[]{:S(2)}, u32[]{:S(2)}) async-start(f32[8,800,128]{2,1,0:T(8,128)} %pad_maximum_fusion), calls=%async_computation.1 | async-start | bytes 6553600 | tf_op jit(solution)/shard_map/all_to_all | solution.py:105
  20.8 2.7 slice_bitcast_fusion.8
  26.1 10.9 %collective-permute-done = s32[1,4,320]{2,1,0:T(4,128)S(1)} collective-permute-done((s32[1,4,320]{2,1,0:T(4,128)S(1)}, s32[1,4,320]{2,1,0:T(4,128)S(1)}, u32[]{:S(2)}, u32[]{:S(2)}) %collective-permute-start) | collective-permute-done | bytes 5152 | tf_op jit(solution)/shard_map/ppermute | solution.py:12
  37.8 27.3 %shard_map.38 = f32[320,2560]{1,0:T(8,128)} custom-call(s32[4,320]{1,0:T(4,128)} %bitcast.200, f32[320,2560]{1,0:T(8,128)} %bitcast.175, f32[8,128,128]{2,1,0:T(8,128)} %bitcast.199), custom_call_target="tpu_custom_call" | custom-call | flops 12582912000 | bytes 6553600 | tf_op jit(solution)/shard_map/pallas_call | solution.py:64
  65.1 3.0 slice_bitcast_fusion.4
  69.3 2.0 fusion.4
  73.2 2.1 reshape.134
  82.3 35.0 %collective-permute-done.3 = f32[8,400,128]{2,1,0:T(8,128)} collective-permute-done((f32[8,400,128]{2,1,0:T(8,128)S(1)}, f32[8,400,128]{2,1,0:T(8,128)}, u32[]{:S(2)}, u32[]{:S(2)}) %collective-permute-start.3) | collective-permute-done | bytes 1638432 | tf_op jit(solution)/shard_map/ppermute | solution.py:12
  117.2 5.4 %all-to-all-start.2 = ((f32[8,400,128]{2,1,0:T(8,128)}), f32[8,400,128]{2,1,0:T(8,128)}, u32[]{:S(2)}, u32[]{:S(2)}) async-start(f32[8,400,128]{2,1,0:T(8,128)} %collective-permute-done.3), calls=%async_computation.2 | async-start | bytes 3276800 | tf_op jit(solution)/shard_map/all_to_all | solution.py:105
  124.6 2.1 reshape.130
  126.7 2.0 copy.102
  147.7 27.3 %shard_map.39 = f32[320,2560]{1,0:T(8,128)} custom-call(s32[4,320]{1,0:T(4,128)} %get-tuple-element.35.codes, f32[320,2560]{1,0:T(8,128)} %pad_maximum_fusion.1.values, f32[8,128,128]{2,1,0:T(8,128)} %get-tuple-element.31.tiles), custom_call_target="tpu_custom_call" | custom-call | flops 12582912000 | bytes 6553600 | tf_op jit(solution)/shard_map/pallas_call | solution.py:64
  174.9 6.0 %all-to-all-start = ((f32[8,400,128]{2,1,0:T(8,128)}), f32[8,400,128]{2,1,0:T(8,128)S(1)}, u32[]{:S(2)}, u32[]{:S(2)}) async-start(f32[8,400,128]{2,1,0:T(8,128)} %collective-permute-done.2), calls=%async_computation | async-start | bytes 3276800 | tf_op jit(solution)/shard_map/all_to_all | solution.py:105
  180.9 3.8 %fusion.1 = (f32[160,2560]{1,0:T(8,128)}, f32[160,2560]{1,0:T(8,128)}) fusion(f32[320,2560]{1,0:T(8,128)} %shard_map.39), kind=kLoop, calls=%fused_computation.34 | loop fusion | bytes 6553600 | tf_op jit(solution)/shard_map/slice | solution.py:160
  184.8 2.5 slice.158
  191.0 2.2 copy.110
  196.0 21.6 %shard_map.40 = f32[160,2560]{1,0:T(8,128)} custom-call(s32[4,320]{1,0:T(4,128)} %get-tuple-element.38.codes, f32[160,2560]{1,0:T(8,128)} %pad_maximum_fusion.4.values, f32[8,128,128]{2,1,0:T(8,128)} %get-tuple-element.34.tiles, f32[160,2560]{1,0:T(8,128)} %get-tuple-element.18.refs_0_), custom_call_target="tpu_custom_call" | custom-call | flops 6291456000 | bytes 3276800 | tf_op jit(solution)/shard_map/pallas_call | solution.py:64
  217.7 2.5 slice_bitcast_fusion.3
  224.2 2.2 copy.118
  228.9 6.0 %all-to-all-start.3 = ((f32[8,400,128]{2,1,0:T(8,128)}), f32[8,400,128]{2,1,0:T(8,128)S(1)}, u32[]{:S(2)}, u32[]{:S(2)}) async-start(f32[8,400,128]{2,1,0:T(8,128)} %pad_maximum_fusion.5), calls=%async_computation.3 | async-start | bytes 3276800 | tf_op jit(solution)/shard_map/all_to_all | solution.py:105
  238.9 2.2 copy.123
  243.8 21.6 %shard_map.41 = f32[160,2560]{1,0:T(8,128)} custom-call(s32[4,320]{1,0:T(4,128)} %get-tuple-element.38.codes, f32[160,2560]{1,0:T(8,128)} %pad_maximum_fusion.6.values, f32[8,128,128]{2,1,0:T(8,128)} %get-tuple-element.34.tiles, f32[160,2560]{1,0:T(8,128)} %get-tuple-element.17.refs_0_), custom_call_target="tpu_custom_call" | custom-call | flops 6291456000 | bytes 3276800 | tf_op jit(solution)/shard_map/pallas_call | solution.py:64
  265.5 2.5 slice_bitcast_fusion.1
  276.6 6.0 %all-to-all-start.4 = ((f32[8,400,128]{2,1,0:T(8,128)}), f32[8,400,128]{2,1,0:T(8,128)S(1)}, u32[]{:S(2)}, u32[]{:S(2)}) async-start(f32[8,400,128]{2,1,0:T(8,128)} %pad_maximum_fusion.7), calls=%async_computation.4 | async-start | bytes 3276800 | tf_op jit(solution)/shard_map/all_to_all | solution.py:105
  282.6 27.3 %shard_map.37 = f32[320,2560]{1,0:T(8,128)} custom-call(s32[4,320]{1,0:T(4,128)} %get-tuple-element.37.codes, f32[320,2560]{1,0:T(8,128)} %bitcast.176, f32[8,128,128]{2,1,0:T(8,128)} %get-tuple-element.33.tiles), custom_call_target="tpu_custom_call" | custom-call | flops 12582912000 | bytes 6553600 | tf_op jit(solution)/shard_map/pallas_call | solution.py:64
  310.6 2.0 copy.128
  312.6 2.2 copy.129
  314.8 2.1 reshape.151
  319.5 2.0 copy.130
  321.5 2.2 copy.131
  323.6 2.1 reshape.154
  329.7 2.1 fusion
  (97 shorter events, 83.6 us)
Async XLA Ops:
  10.6 1.0 copy-start.5
  13.5 103.7 %all-to-all-start.1 = ((f32[8,800,128]{2,1,0:T(8,128)}), f32[8,800,128]{2,1,0:T(8,128)S(1)}, u32[]{:S(2)}, u32[]{:S(2)}) async-start(f32[8,800,128]{2,1,0:T(8,128)} %pad_maximum_fusion), calls=%async_computation.1 | async-start | bytes 6553600 | tf_op jit(solution)/shard_map/all_to_all | solution.py:105
  20.8 4.2 %copy-start.9 = (s32[1,4,4,320]{3,2,1,0:T(4,128)S(1)}, s32[1,4,4,320]{3,2,1,0:T(4,128)}, u32[]{:S(2)}) copy-start(s32[1,4,4,320]{3,2,1,0:T(4,128)} %param.4) | copy-start | bytes 61444
  23.5 13.5 %collective-permute-start.1 = (f32[1,8,128,128]{3,2,1,0:T(8,128)S(1)}, f32[1,8,128,128]{3,2,1,0:T(8,128)S(1)}, u32[]{:S(2)}, u32[]{:S(2)}) collective-permute-start(f32[1,8,128,128]{3,2,1,0:T(8,128)S(1)} %get-tuple-element.32), channel_id=1, source_target_pairs={{0,2},{1,3},{2,0},{3,1},{4,6},{5,7},{6,4},{7,5},{8,10},{9,11},{10,... | collective-permute-start | bytes 1572872 | tf_op jit(solution)/shard_map/ppermute | solution.py:12
  25.6 11.4 %collective-permute-start = (s32[1,4,320]{2,1,0:T(4,128)S(1)}, s32[1,4,320]{2,1,0:T(4,128)S(1)}, u32[]{:S(2)}, u32[]{:S(2)}) collective-permute-start(s32[1,4,320]{2,1,0:T(4,128)S(1)} %get-tuple-element.36), channel_id=1, source_target_pairs={{0,2},{1,3},{2,0},{3,1},{4,6},{5,7},{6,4},{7,5},{8,10},{9,11},{10,... | collective-permute-start | bytes 15368 | tf_op jit(solution)/shard_map/ppermute | solution.py:12
  37.0 0.6 copy-start.11
  37.0 0.8 copy-start.10
  80.7 36.5 %collective-permute-start.3 = (f32[8,400,128]{2,1,0:T(8,128)S(1)}, f32[8,400,128]{2,1,0:T(8,128)}, u32[]{:S(2)}, u32[]{:S(2)}) collective-permute-start(f32[8,400,128]{2,1,0:T(8,128)S(1)} %pad_maximum_fusion.3), channel_id=1, source_target_pairs={{0,2},{1,3},{2,0},{3,1},{4,6},{5,7},{6,4},{7,5},{8,10},{9,11},{10,... | collective-permute-start | bytes 4915208 | tf_op jit(solution)/shard_map/ppermute | solution.py:12
  117.2 57.7 %all-to-all-start.2 = ((f32[8,400,128]{2,1,0:T(8,128)}), f32[8,400,128]{2,1,0:T(8,128)}, u32[]{:S(2)}, u32[]{:S(2)}) async-start(f32[8,400,128]{2,1,0:T(8,128)} %collective-permute-done.3), calls=%async_computation.2 | async-start | bytes 3276800 | tf_op jit(solution)/shard_map/all_to_all | solution.py:105
  130.6 1.5 copy-start.8
  133.4 41.5 %collective-permute-start.2 = (f32[8,400,128]{2,1,0:T(8,128)}, f32[8,400,128]{2,1,0:T(8,128)}, u32[]{:S(2)}, u32[]{:S(2)}) collective-permute-start(f32[8,400,128]{2,1,0:T(8,128)} %pad_maximum_fusion.2), channel_id=1, source_target_pairs={{0,2},{1,3},{2,0},{3,1},{4,6},{5,7},{6,4},{7,5},{8,10},{9,11},{10,... | collective-permute-start | bytes 4915208 | tf_op jit(solution)/shard_map/ppermute | solution.py:12
  137.6 1.8 copy-start.1
  139.4 1.5 copy-start.7
  141.4 4.3 %copy-start.2 = (f32[2560,128]{0,1:T(8,128)S(1)}, f32[2560,128]{0,1:T(8,128)}, u32[]{:S(2)}) copy-start(f32[2560,128]{0,1:T(8,128)} %copy.114) | copy-start | bytes 3932164
  174.9 54.0 %all-to-all-start = ((f32[8,400,128]{2,1,0:T(8,128)}), f32[8,400,128]{2,1,0:T(8,128)S(1)}, u32[]{:S(2)}, u32[]{:S(2)}) async-start(f32[8,400,128]{2,1,0:T(8,128)} %collective-permute-done.2), calls=%async_computation | async-start | bytes 3276800 | tf_op jit(solution)/shard_map/all_to_all | solution.py:105
  228.9 6.0 %copy-start = (f32[8,400,128]{2,1,0:T(8,128)}, f32[8,400,128]{2,1,0:T(8,128)S(1)}, u32[]{:S(2)}) copy-start(f32[8,400,128]{2,1,0:T(8,128)S(1)} %all-to-all-done) | copy-start | bytes 4915204
  228.9 47.6 %all-to-all-start.3 = ((f32[8,400,128]{2,1,0:T(8,128)}), f32[8,400,128]{2,1,0:T(8,128)S(1)}, u32[]{:S(2)}, u32[]{:S(2)}) async-start(f32[8,400,128]{2,1,0:T(8,128)} %pad_maximum_fusion.5), calls=%async_computation.3 | async-start | bytes 3276800 | tf_op jit(solution)/shard_map/all_to_all | solution.py:105
  236.1 1.8 slice-start
  276.6 42.1 %all-to-all-start.4 = ((f32[8,400,128]{2,1,0:T(8,128)}), f32[8,400,128]{2,1,0:T(8,128)S(1)}, u32[]{:S(2)}, u32[]{:S(2)}) async-start(f32[8,400,128]{2,1,0:T(8,128)} %pad_maximum_fusion.7), calls=%async_computation.4 | async-start | bytes 3276800 | tf_op jit(solution)/shard_map/all_to_all | solution.py:105
  327.6 1.9 copy-start.3
  327.7 1.8 copy-start.4
  327.8 1.9 copy-start.6

commit v3 on v2

--- a/solution.py
+++ b/solution.py
@@ -146,11 +146,12 @@
     sent = exchange(packed)
     length = sent.shape[1] // parts
     mixed = apply_operator(own, partner_codes, partner_tiles)
-    crossing = [from_partner(outgoing(mixed, p), "irrep", bit) for p in range(parts)]
-    sent, crossing[0] = lax.optimization_barrier((sent, crossing[0]))
+    leaving = [outgoing(mixed, p) for p in range(parts)]
+    crossing = [from_partner(x, "irrep", bit) for x in leaving]
     columns = jnp.concatenate(
         [by_beta(sent[:, p * length : (p + 1) * length]) for p in range(parts)], axis=0
     )
+    crossing[0] = lax.optimization_barrier((crossing[0], columns, leaving))[0]
     beta_term = apply_operator(own, codes[0], bank[0])
     alpha_own = apply_operator(columns, codes[1], bank[1])
     crossed = [exchange(x) for x in crossing]

time: 334 us -> 319 us (0.955)
  waiting for transfers between devices: 45.9 us -> 27 us
  local copies, waits for them, and re-layouts: 111 us -> 115 us
    ppermute x4, waiting for transfers between devices: 45.9 us -> 25.2 us  [from_partner(): lax.ppermute(shard, axis, [(i, i ^ 1 << bit) for i in range(lax.axis_size...]
    reshape x4, local copies, waits for them, and re-layouts: 6.75 us -> 10.1 us  [by_beta(): x.reshape(count * rows, x.shape[-1])]
    unnamed x26 -> x28, local copies, waits for them, and re-layouts: 8.18 us -> 8.27 us
  transfers between devices with their start and end apart: 9 -> 9, of which waited for: 2 -> 6; matrix products, arithmetic and copies ran while one was open for 29% -> 32% of each run, Pallas kernels for 38% -> 39%
where the time goes in v3:
time: 319 us; the launch traced here: 317 us
  Pallas kernels  125 us (39%)
  local copies, waits for them, and re-layouts  115 us (36%)
  starting transfers between devices  34.2 us (11%)
  waiting for transfers between devices  27 us (8%)
  other arithmetic  15.3 us (5%)
    pallas_call x5, Pallas kernels, apply_operator(): pl.pallas_call(operator_kernel, out_shape=jax.ShapeDtypeStruct((rows, ext...  125 us
    all_to_all x5, starting transfers between devices, exchange(): lax.all_to_all(packed, 'rows', split_axis=0, concat_axis=0, tiled=True)  29.2 us
    ppermute x4, waiting for transfers between devices, from_partner(): lax.ppermute(shard, axis, [(i, i ^ 1 << bit) for i in range(lax.axis_size...  25.2 us
    slice x12, local copies, waits for them, and re-layouts, split(): rest = unfold(packed[:, rows if wide else 0:], narrow) if narrow else None  12.8 us
    reshape x8, local copies, waits for them, and re-layouts, fold(): folded = blocks.reshape(count, times, rows // times, narrow)  10.4 us
    transpose x6, local copies, waits for them, and re-layouts, unfold(): jnp.swapaxes(folded, 1, 2).reshape(count, rows * (width // narrow), narrow)  10.3 us
    reshape x4, local copies, waits for them, and re-layouts, by_beta(): x.reshape(count * rows, x.shape[-1])  10.1 us
    reshape x6, local copies, waits for them, and re-layouts, fold(): return jnp.swapaxes(folded, 1, 2).reshape(count, rows // times, width)  9.54 us
  transfers between devices with their start and end apart: 9, of which 6 were waited for; matrix products, arithmetic and copies ran while one was open for 32% of the time, Pallas kernels for 39%

profile of v3, /device:TPU:0, one launch (start us, length us, event | category | flops | bytes accessed | tf_op | source)
XLA Modules:
  0.0 316.9 jit_solution(11558150609446740916)
XLA Ops:
  13.5 7.3 %all-to-all-start.1 = ((f32[8,800,128]{2,1,0:T(8,128)}), f32[8,800,128]{2,1,0:T(8,128)S(1)}, u32[]{:S(2)}, u32[]{:S(2)}) async-start(f32[8,800,128]{2,1,0:T(8,128)} %pad_maximum_fusion), calls=%async_computation.1 | async-start | bytes 6553600 | tf_op jit(solution)/shard_map/all_to_all | solution.py:105
  20.8 2.7 slice_bitcast_fusion.8
  26.2 10.9 %collective-permute-done = s32[1,4,320]{2,1,0:T(4,128)S(1)} collective-permute-done((s32[1,4,320]{2,1,0:T(4,128)S(1)}, s32[1,4,320]{2,1,0:T(4,128)S(1)}, u32[]{:S(2)}, u32[]{:S(2)}) %collective-permute-start) | collective-permute-done | bytes 5152 | tf_op jit(solution)/shard_map/ppermute | solution.py:12
  37.9 27.3 %shard_map.38 = f32[320,2560]{1,0:T(8,128)} custom-call(s32[4,320]{1,0:T(4,128)} %bitcast.200, f32[320,2560]{1,0:T(8,128)} %bitcast.175, f32[8,128,128]{2,1,0:T(8,128)} %bitcast.199), custom_call_target="tpu_custom_call" | custom-call | flops 12582912000 | bytes 6553600 | tf_op jit(solution)/shard_map/pallas_call | solution.py:64
  65.2 3.1 slice_bitcast_fusion.4
  73.3 2.1 reshape.134
  79.3 2.8 pad_maximum_fusion.3
  85.5 2.1 reshape.130
  96.1 2.8 copy.108
  98.9 2.8 copy.111
  110.6 8.2 %collective-permute-done.3 = f32[8,400,128]{2,1,0:T(8,128)} collective-permute-done((f32[8,400,128]{2,1,0:T(8,128)}, f32[8,400,128]{2,1,0:T(8,128)}, u32[]{:S(2)}, u32[]{:S(2)}) %collective-permute-start.3) | collective-permute-done | bytes 1638432 | tf_op jit(solution)/shard_map/ppermute | solution.py:12
  118.8 5.4 %all-to-all-start.2 = ((f32[8,400,128]{2,1,0:T(8,128)}), f32[8,400,128]{2,1,0:T(8,128)S(1)}, u32[]{:S(2)}, u32[]{:S(2)}) async-start(f32[8,400,128]{2,1,0:T(8,128)} %collective-permute-done.3), calls=%async_computation.2 | async-start | bytes 3276800 | tf_op jit(solution)/shard_map/all_to_all | solution.py:105
  125.7 27.3 %shard_map.39 = f32[320,2560]{1,0:T(8,128)} custom-call(s32[4,320]{1,0:T(4,128)} %get-tuple-element.33.codes, f32[320,2560]{1,0:T(8,128)} %pad_maximum_fusion.1.values, f32[8,128,128]{2,1,0:T(8,128)} %get-tuple-element.29.tiles), custom_call_target="tpu_custom_call" | custom-call | flops 12582912000 | bytes 6553600 | tf_op jit(solution)/shard_map/pallas_call | solution.py:64
  153.1 6.1 %collective-permute-done.2 = f32[8,400,128]{2,1,0:T(8,128)} collective-permute-done((f32[8,400,128]{2,1,0:T(8,128)S(1)}, f32[8,400,128]{2,1,0:T(8,128)}, u32[]{:S(2)}, u32[]{:S(2)}) %collective-permute-start.2) | collective-permute-done | bytes 1638432 | tf_op jit(solution)/shard_map/ppermute | solution.py:12
  160.4 4.5 %all-to-all-start = ((f32[8,400,128]{2,1,0:T(8,128)}), f32[8,400,128]{2,1,0:T(8,128)S(1)}, u32[]{:S(2)}, u32[]{:S(2)}) async-start(f32[8,400,128]{2,1,0:T(8,128)} %collective-permute-done.2), calls=%async_computation | async-start | bytes 3276800 | tf_op jit(solution)/shard_map/all_to_all | solution.py:105
  164.9 3.8 %fusion.1 = (f32[160,2560]{1,0:T(8,128)}, f32[160,2560]{1,0:T(8,128)}) fusion(f32[320,2560]{1,0:T(8,128)} %shard_map.39), kind=kLoop, calls=%fused_computation.34 | loop fusion | bytes 6553600 | tf_op jit(solution)/shard_map/slice | solution.py:161
  169.9 2.8 copy.114
  173.4 2.1 copy.115
  175.5 2.2 copy.116
  180.6 21.6 %shard_map.40 = f32[160,2560]{1,0:T(8,128)} custom-call(s32[4,320]{1,0:T(4,128)} %get-tuple-element.36.codes, f32[160,2560]{1,0:T(8,128)} %pad_maximum_fusion.4.values, f32[8,128,128]{2,1,0:T(8,128)} %get-tuple-element.32.tiles, f32[160,2560]{1,0:T(8,128)} %get-tuple-element.16.refs_0_), custom_call_target="tpu_custom_call" | custom-call | flops 6291456000 | bytes 3276800 | tf_op jit(solution)/shard_map/pallas_call | solution.py:64
  202.2 2.5 slice_bitcast_fusion.3
  208.7 2.1 copy.118
  213.5 6.0 %all-to-all-start.3 = ((f32[8,400,128]{2,1,0:T(8,128)}), f32[8,400,128]{2,1,0:T(8,128)S(1)}, u32[]{:S(2)}, u32[]{:S(2)}) async-start(f32[8,400,128]{2,1,0:T(8,128)} %pad_maximum_fusion.5), calls=%async_computation.3 | async-start | bytes 3276800 | tf_op jit(solution)/shard_map/all_to_all | solution.py:105
  223.4 2.2 copy.123
  228.4 21.6 %shard_map.41 = f32[160,2560]{1,0:T(8,128)} custom-call(s32[4,320]{1,0:T(4,128)} %get-tuple-element.36.codes, f32[160,2560]{1,0:T(8,128)} %pad_maximum_fusion.6.values, f32[8,128,128]{2,1,0:T(8,128)} %get-tuple-element.32.tiles, f32[160,2560]{1,0:T(8,128)} %get-tuple-element.15.refs_0_), custom_call_target="tpu_custom_call" | custom-call | flops 6291456000 | bytes 3276800 | tf_op jit(solution)/shard_map/pallas_call | solution.py:64
  250.0 2.5 slice_bitcast_fusion.1
  261.1 6.0 %all-to-all-start.4 = ((f32[8,400,128]{2,1,0:T(8,128)}), f32[8,400,128]{2,1,0:T(8,128)S(1)}, u32[]{:S(2)}, u32[]{:S(2)}) async-start(f32[8,400,128]{2,1,0:T(8,128)} %pad_maximum_fusion.7), calls=%async_computation.4 | async-start | bytes 3276800 | tf_op jit(solution)/shard_map/all_to_all | solution.py:105
  267.1 27.3 %shard_map.37 = f32[320,2560]{1,0:T(8,128)} custom-call(s32[4,320]{1,0:T(4,128)} %get-tuple-element.35.codes, f32[320,2560]{1,0:T(8,128)} %bitcast.176, f32[8,128,128]{2,1,0:T(8,128)} %get-tuple-element.31.tiles), custom_call_target="tpu_custom_call" | custom-call | flops 12582912000 | bytes 6553600 | tf_op jit(solution)/shard_map/pallas_call | solution.py:64
  297.1 2.2 copy.129
  306.5 2.2 copy.131
  308.7 2.1 reshape.154
  314.7 2.1 fusion
  (99 shorter events, 89.9 us)
Async XLA Ops:
  10.6 1.0 copy-start.7
  13.5 80.8 %all-to-all-start.1 = ((f32[8,800,128]{2,1,0:T(8,128)}), f32[8,800,128]{2,1,0:T(8,128)S(1)}, u32[]{:S(2)}, u32[]{:S(2)}) async-start(f32[8,800,128]{2,1,0:T(8,128)} %pad_maximum_fusion), calls=%async_computation.1 | async-start | bytes 6553600 | tf_op jit(solution)/shard_map/all_to_all | solution.py:105
  20.8 4.2 %copy-start.10 = (s32[1,4,4,320]{3,2,1,0:T(4,128)S(1)}, s32[1,4,4,320]{3,2,1,0:T(4,128)}, u32[]{:S(2)}) copy-start(s32[1,4,4,320]{3,2,1,0:T(4,128)} %param.4) | copy-start | bytes 61444
  23.6 13.5 %collective-permute-start.1 = (f32[1,8,128,128]{3,2,1,0:T(8,128)S(1)}, f32[1,8,128,128]{3,2,1,0:T(8,128)S(1)}, u32[]{:S(2)}, u32[]{:S(2)}) collective-permute-start(f32[1,8,128,128]{3,2,1,0:T(8,128)S(1)} %get-tuple-element.30), channel_id=1, source_target_pairs={{0,2},{1,3},{2,0},{3,1},{4,6},{5,7},{6,4},{7,5},{8,10},{9,11},{10,... | collective-permute-start | bytes 1572872 | tf_op jit(solution)/shard_map/ppermute | solution.py:12
  25.7 11.4 %collective-permute-start = (s32[1,4,320]{2,1,0:T(4,128)S(1)}, s32[1,4,320]{2,1,0:T(4,128)S(1)}, u32[]{:S(2)}, u32[]{:S(2)}) collective-permute-start(s32[1,4,320]{2,1,0:T(4,128)S(1)} %get-tuple-element.34), channel_id=1, source_target_pairs={{0,2},{1,3},{2,0},{3,1},{4,6},{5,7},{6,4},{7,5},{8,10},{9,11},{10,... | collective-permute-start | bytes 15368 | tf_op jit(solution)/shard_map/ppermute | solution.py:12
  37.1 0.6 copy-start.12
  37.1 0.8 copy-start.11
  82.1 36.6 %collective-permute-start.3 = (f32[8,400,128]{2,1,0:T(8,128)}, f32[8,400,128]{2,1,0:T(8,128)}, u32[]{:S(2)}, u32[]{:S(2)}) collective-permute-start(f32[8,400,128]{2,1,0:T(8,128)} %pad_maximum_fusion.3), channel_id=1, source_target_pairs={{0,2},{1,3},{2,0},{3,1},{4,6},{5,7},{6,4},{7,5},{8,10},{9,11},{10,... | collective-permute-start | bytes 4915208 | tf_op jit(solution)/shard_map/ppermute | solution.py:12
  91.5 1.5 copy-start.9
  104.1 4.5 %copy-start.2 = (f32[2560,128]{0,1:T(8,128)S(1)}, f32[2560,128]{0,1:T(8,128)}, u32[]{:S(2)}) copy-start(f32[2560,128]{0,1:T(8,128)} %copy.108) | copy-start | bytes 3932164
  104.1 4.5 %copy-start.3 = (f32[2560,128]{0,1:T(8,128)S(1)}, f32[2560,128]{0,1:T(8,128)}, u32[]{:S(2)}) copy-start(f32[2560,128]{0,1:T(8,128)} %copy.111) | copy-start | bytes 3932164
  110.6 13.6 %copy-start.5 = (f32[8,400,128]{2,1,0:T(8,128)S(1)}, f32[8,400,128]{2,1,0:T(8,128)}, u32[]{:S(2)}) copy-start(f32[8,400,128]{2,1,0:T(8,128)} %pad_maximum_fusion.2) | copy-start | bytes 4915204
  118.8 41.7 %all-to-all-start.2 = ((f32[8,400,128]{2,1,0:T(8,128)}), f32[8,400,128]{2,1,0:T(8,128)S(1)}, u32[]{:S(2)}, u32[]{:S(2)}) async-start(f32[8,400,128]{2,1,0:T(8,128)} %collective-permute-done.3), calls=%async_computation.2 | async-start | bytes 3276800 | tf_op jit(solution)/shard_map/all_to_all | solution.py:105
  124.2 35.0 %collective-permute-start.2 = (f32[8,400,128]{2,1,0:T(8,128)S(1)}, f32[8,400,128]{2,1,0:T(8,128)}, u32[]{:S(2)}, u32[]{:S(2)}) collective-permute-start(f32[8,400,128]{2,1,0:T(8,128)S(1)} %copy-done.5), channel_id=1, source_target_pairs={{0,2},{1,3},{2,0},{3,1},{4,6},{5,7},{6,4},{7,5},{8,10},{9,11},{10,... | collective-permute-start | bytes 4915208 | tf_op jit(solution)/shard_map/ppermute | solution.py:12
  160.4 53.1 %all-to-all-start = ((f32[8,400,128]{2,1,0:T(8,128)}), f32[8,400,128]{2,1,0:T(8,128)S(1)}, u32[]{:S(2)}, u32[]{:S(2)}) async-start(f32[8,400,128]{2,1,0:T(8,128)} %collective-permute-done.2), calls=%async_computation | async-start | bytes 3276800 | tf_op jit(solution)/shard_map/all_to_all | solution.py:105
  173.4 5.8 %copy-start.1 = (f32[2560,128]{0,1:T(8,128)S(1)}, f32[2560,128]{0,1:T(8,128)}, u32[]{:S(2)}) copy-start(f32[2560,128]{0,1:T(8,128)} %copy.114) | copy-start | bytes 3932164
  213.5 6.0 %copy-start = (f32[8,400,128]{2,1,0:T(8,128)}, f32[8,400,128]{2,1,0:T(8,128)S(1)}, u32[]{:S(2)}) copy-start(f32[8,400,128]{2,1,0:T(8,128)S(1)} %all-to-all-done) | copy-start | bytes 4915204
  213.5 47.7 %all-to-all-start.3 = ((f32[8,400,128]{2,1,0:T(8,128)}), f32[8,400,128]{2,1,0:T(8,128)S(1)}, u32[]{:S(2)}, u32[]{:S(2)}) async-start(f32[8,400,128]{2,1,0:T(8,128)} %pad_maximum_fusion.5), calls=%async_computation.3 | async-start | bytes 3276800 | tf_op jit(solution)/shard_map/all_to_all | solution.py:105
  220.6 1.8 slice-start
  261.1 42.7 %all-to-all-start.4 = ((f32[8,400,128]{2,1,0:T(8,128)}), f32[8,400,128]{2,1,0:T(8,128)S(1)}, u32[]{:S(2)}, u32[]{:S(2)}) async-start(f32[8,400,128]{2,1,0:T(8,128)} %pad_maximum_fusion.7), calls=%async_computation.4 | async-start | bytes 3276800 | tf_op jit(solution)/shard_map/all_to_all | solution.py:105
  312.7 1.9 copy-start.4
  312.8 1.8 copy-start.6
  312.8 1.9 copy-start.8

commit v4 on v3

--- a/solution.py
+++ b/solution.py
@@ -169,8 +169,11 @@
 
 def body(coefficients, block_codes, tile_bank):
     bit = lax.axis_size("irrep").bit_length() - 2
-    partner_tiles = from_partner(tile_bank[:, 3], "irrep", bit)
-    partner_codes = from_partner(block_codes[:, 3], "irrep", bit)
+    tiles, codes, coefficients = lax.optimization_barrier(
+        (tile_bank[:, 3], block_codes[:, 3], coefficients)
+    )
+    partner_tiles = from_partner(tiles, "irrep", bit)
+    partner_codes = from_partner(codes, "irrep", bit)
     return jnp.stack(
         [
             one_irrep(

time: 319 us -> 318 us (level)
  transfers between devices with their start and end apart: 9 -> 9, of which waited for: 6 -> 6; matrix products, arithmetic and copies ran while one was open for 32% -> 31% of each run, Pallas kernels for 39% -> 40%
where the time goes in v4:
time: 318 us; the launch traced here: 316 us
  Pallas kernels  125 us (39%)
  local copies, waits for them, and re-layouts  113 us (36%)
  starting transfers between devices  34.2 us (11%)
  waiting for transfers between devices  27.8 us (9%)
  other arithmetic  15.3 us (5%)
    pallas_call x5, Pallas kernels, apply_operator(): pl.pallas_call(operator_kernel, out_shape=jax.ShapeDtypeStruct((rows, ext...  125 us
    all_to_all x5, starting transfers between devices, exchange(): lax.all_to_all(packed, 'rows', split_axis=0, concat_axis=0, tiled=True)  29.2 us
    ppermute x4, waiting for transfers between devices, from_partner(): lax.ppermute(shard, axis, [(i, i ^ 1 << bit) for i in range(lax.axis_size...  23.4 us
    slice x12, local copies, waits for them, and re-layouts, split(): rest = unfold(packed[:, rows if wide else 0:], narrow) if narrow else None  12.8 us
    reshape x8, local copies, waits for them, and re-layouts, fold(): folded = blocks.reshape(count, times, rows // times, narrow)  10.4 us
    transpose x6, local copies, waits for them, and re-layouts, unfold(): jnp.swapaxes(folded, 1, 2).reshape(count, rows * (width // narrow), narrow)  10.3 us
    reshape x4, local copies, waits for them, and re-layouts, by_beta(): x.reshape(count * rows, x.shape[-1])  10.2 us
    reshape x6, local copies, waits for them, and re-layouts, fold(): return jnp.swapaxes(folded, 1, 2).reshape(count, rows // times, width)  9.52 us
  transfers between devices with their start and end apart: 9, of which 6 were waited for; matrix products, arithmetic and copies ran while one was open for 31% of the time, Pallas kernels for 40%

profile of v4, /device:TPU:0, one launch (start us, length us, event | category | flops | bytes accessed | tf_op | source)
XLA Modules:
  0.0 315.9 jit_solution(12943528712083973811)
XLA Ops:
  1.3 3.0 slice_bitcast_fusion.8
  15.2 7.3 %all-to-all-start.1 = ((f32[8,800,128]{2,1,0:T(8,128)}), f32[8,800,128]{2,1,0:T(8,128)S(1)}, u32[]{:S(2)}, u32[]{:S(2)}) async-start(f32[8,800,128]{2,1,0:T(8,128)} %pad_maximum_fusion), calls=%async_computation.1 | async-start | bytes 6553600 | tf_op jit(solution)/shard_map/all_to_all | solution.py:105
  24.5 11.7 %collective-permute-done = s32[1,4,320]{2,1,0:T(4,128)S(1)} collective-permute-done((s32[1,4,320]{2,1,0:T(4,128)S(1)}, s32[1,4,320]{2,1,0:T(4,128)S(1)}, u32[]{:S(2)}, u32[]{:S(2)}) %collective-permute-start) | collective-permute-done | bytes 5152 | tf_op jit(solution)/shard_map/ppermute | solution.py:12
  37.0 27.3 %shard_map.38 = f32[320,2560]{1,0:T(8,128)} custom-call(s32[4,320]{1,0:T(4,128)} %bitcast.200, f32[320,2560]{1,0:T(8,128)} %bitcast.173, f32[8,128,128]{2,1,0:T(8,128)} %bitcast.199), custom_call_target="tpu_custom_call" | custom-call | flops 12582912000 | bytes 6553600 | tf_op jit(solution)/shard_map/pallas_call | solution.py:64
  64.3 3.1 slice_bitcast_fusion.4
  72.3 2.1 reshape.134
  78.3 2.8 pad_maximum_fusion.3
  84.5 2.1 reshape.130
  93.2 2.7 all-to-all-done.1
  97.8 2.8 copy.108
  100.6 2.8 copy.111
  112.2 5.5 %collective-permute-done.3 = f32[8,400,128]{2,1,0:T(8,128)} collective-permute-done((f32[8,400,128]{2,1,0:T(8,128)}, f32[8,400,128]{2,1,0:T(8,128)}, u32[]{:S(2)}, u32[]{:S(2)}) %collective-permute-start.3) | collective-permute-done | bytes 1638432 | tf_op jit(solution)/shard_map/ppermute | solution.py:12
  117.7 5.4 %all-to-all-start.2 = ((f32[8,400,128]{2,1,0:T(8,128)}), f32[8,400,128]{2,1,0:T(8,128)S(1)}, u32[]{:S(2)}, u32[]{:S(2)}) async-start(f32[8,400,128]{2,1,0:T(8,128)} %collective-permute-done.3), calls=%async_computation.2 | async-start | bytes 3276800 | tf_op jit(solution)/shard_map/all_to_all | solution.py:105
  124.7 27.3 %shard_map.39 = f32[320,2560]{1,0:T(8,128)} custom-call(s32[4,320]{1,0:T(4,128)} %get-tuple-element.39.codes, f32[320,2560]{1,0:T(8,128)} %pad_maximum_fusion.1.values, f32[8,128,128]{2,1,0:T(8,128)} %get-tuple-element.35.tiles), custom_call_target="tpu_custom_call" | custom-call | flops 12582912000 | bytes 6553600 | tf_op jit(solution)/shard_map/pallas_call | solution.py:64
  152.0 6.2 %collective-permute-done.2 = f32[8,400,128]{2,1,0:T(8,128)} collective-permute-done((f32[8,400,128]{2,1,0:T(8,128)S(1)}, f32[8,400,128]{2,1,0:T(8,128)}, u32[]{:S(2)}, u32[]{:S(2)}) %collective-permute-start.2) | collective-permute-done | bytes 1638432 | tf_op jit(solution)/shard_map/ppermute | solution.py:12
  159.4 4.5 %all-to-all-start = ((f32[8,400,128]{2,1,0:T(8,128)}), f32[8,400,128]{2,1,0:T(8,128)S(1)}, u32[]{:S(2)}, u32[]{:S(2)}) async-start(f32[8,400,128]{2,1,0:T(8,128)} %collective-permute-done.2), calls=%async_computation | async-start | bytes 3276800 | tf_op jit(solution)/shard_map/all_to_all | solution.py:105
  163.8 3.8 %fusion.1 = (f32[160,2560]{1,0:T(8,128)}, f32[160,2560]{1,0:T(8,128)}) fusion(f32[320,2560]{1,0:T(8,128)} %shard_map.39), kind=kLoop, calls=%fused_computation.34 | loop fusion | bytes 6553600 | tf_op jit(solution)/shard_map/slice | solution.py:161
  168.8 2.8 copy.114
  172.4 2.1 copy.115
  174.5 2.2 copy.116
  179.5 21.7 %shard_map.40 = f32[160,2560]{1,0:T(8,128)} custom-call(s32[4,320]{1,0:T(4,128)} %get-tuple-element.42.codes, f32[160,2560]{1,0:T(8,128)} %pad_maximum_fusion.4.values, f32[8,128,128]{2,1,0:T(8,128)} %get-tuple-element.38.tiles, f32[160,2560]{1,0:T(8,128)} %get-tuple-element.22.refs_0_), custom_call_target="tpu_custom_call" | custom-call | flops 6291456000 | bytes 3276800 | tf_op jit(solution)/shard_map/pallas_call | solution.py:64
  201.2 2.5 slice_bitcast_fusion.3
  207.8 2.2 copy.118
  212.5 6.0 %all-to-all-start.3 = ((f32[8,400,128]{2,1,0:T(8,128)}), f32[8,400,128]{2,1,0:T(8,128)S(1)}, u32[]{:S(2)}, u32[]{:S(2)}) async-start(f32[8,400,128]{2,1,0:T(8,128)} %pad_maximum_fusion.5), calls=%async_computation.3 | async-start | bytes 3276800 | tf_op jit(solution)/shard_map/all_to_all | solution.py:105
  222.4 2.2 copy.123
  227.4 21.6 %shard_map.41 = f32[160,2560]{1,0:T(8,128)} custom-call(s32[4,320]{1,0:T(4,128)} %get-tuple-element.42.codes, f32[160,2560]{1,0:T(8,128)} %pad_maximum_fusion.6.values, f32[8,128,128]{2,1,0:T(8,128)} %get-tuple-element.38.tiles, f32[160,2560]{1,0:T(8,128)} %get-tuple-element.21.refs_0_), custom_call_target="tpu_custom_call" | custom-call | flops 6291456000 | bytes 3276800 | tf_op jit(solution)/shard_map/pallas_call | solution.py:64
  249.0 2.5 slice_bitcast_fusion.1
  260.1 6.0 %all-to-all-start.4 = ((f32[8,400,128]{2,1,0:T(8,128)}), f32[8,400,128]{2,1,0:T(8,128)S(1)}, u32[]{:S(2)}, u32[]{:S(2)}) async-start(f32[8,400,128]{2,1,0:T(8,128)} %pad_maximum_fusion.7), calls=%async_computation.4 | async-start | bytes 3276800 | tf_op jit(solution)/shard_map/all_to_all | solution.py:105
  266.1 27.3 %shard_map.37 = f32[320,2560]{1,0:T(8,128)} custom-call(s32[4,320]{1,0:T(4,128)} %get-tuple-element.41.codes, f32[320,2560]{1,0:T(8,128)} %bitcast.174, f32[8,128,128]{2,1,0:T(8,128)} %get-tuple-element.36.tiles), custom_call_target="tpu_custom_call" | custom-call | flops 12582912000 | bytes 6553600 | tf_op jit(solution)/shard_map/pallas_call | solution.py:64
  296.1 2.2 copy.129
  305.5 2.2 copy.131
  313.7 2.1 fusion
  (99 shorter events, 89.7 us)
Async XLA Ops:
  1.3 3.0 copy-start.4
  12.2 1.0 copy-start.8
  15.2 80.8 %all-to-all-start.1 = ((f32[8,800,128]{2,1,0:T(8,128)}), f32[8,800,128]{2,1,0:T(8,128)S(1)}, u32[]{:S(2)}, u32[]{:S(2)}) async-start(f32[8,800,128]{2,1,0:T(8,128)} %pad_maximum_fusion), calls=%async_computation.1 | async-start | bytes 6553600 | tf_op jit(solution)/shard_map/all_to_all | solution.py:105
  22.4 13.7 %collective-permute-start.1 = (f32[1,8,128,128]{3,2,1,0:T(8,128)}, f32[1,8,128,128]{3,2,1,0:T(8,128)S(1)}, u32[]{:S(2)}, u32[]{:S(2)}) collective-permute-start(f32[1,8,128,128]{3,2,1,0:T(8,128)} %get-tuple-element.16), channel_id=1, source_target_pairs={{0,2},{1,3},{2,0},{3,1},{4,6},{5,7},{6,4},{7,5},{8,10},{9,11},{10,... | collective-permute-start | bytes 1572872 | tf_op jit(solution)/shard_map/ppermute | solution.py:12
  23.9 12.2 %collective-permute-start = (s32[1,4,320]{2,1,0:T(4,128)S(1)}, s32[1,4,320]{2,1,0:T(4,128)S(1)}, u32[]{:S(2)}, u32[]{:S(2)}) collective-permute-start(s32[1,4,320]{2,1,0:T(4,128)S(1)} %get-tuple-element.15), channel_id=1, source_target_pairs={{0,2},{1,3},{2,0},{3,1},{4,6},{5,7},{6,4},{7,5},{8,10},{9,11},{10,... | collective-permute-start | bytes 15368 | tf_op jit(solution)/shard_map/ppermute | solution.py:12
  36.2 0.6 copy-start.12
  36.2 0.8 copy-start.11
  81.1 36.7 %collective-permute-start.3 = (f32[8,400,128]{2,1,0:T(8,128)}, f32[8,400,128]{2,1,0:T(8,128)}, u32[]{:S(2)}, u32[]{:S(2)}) collective-permute-start(f32[8,400,128]{2,1,0:T(8,128)} %pad_maximum_fusion.3), channel_id=1, source_target_pairs={{0,2},{1,3},{2,0},{3,1},{4,6},{5,7},{6,4},{7,5},{8,10},{9,11},{10,... | collective-permute-start | bytes 4915208 | tf_op jit(solution)/shard_map/ppermute | solution.py:12
  90.4 1.5 copy-start.10
  105.7 4.5 %copy-start.2 = (f32[2560,128]{0,1:T(8,128)S(1)}, f32[2560,128]{0,1:T(8,128)}, u32[]{:S(2)}) copy-start(f32[2560,128]{0,1:T(8,128)} %copy.108) | copy-start | bytes 3932164
  105.8 4.5 %copy-start.3 = (f32[2560,128]{0,1:T(8,128)S(1)}, f32[2560,128]{0,1:T(8,128)}, u32[]{:S(2)}) copy-start(f32[2560,128]{0,1:T(8,128)} %copy.111) | copy-start | bytes 3932164
  112.2 10.9 %copy-start.6 = (f32[8,400,128]{2,1,0:T(8,128)S(1)}, f32[8,400,128]{2,1,0:T(8,128)}, u32[]{:S(2)}) copy-start(f32[8,400,128]{2,1,0:T(8,128)} %pad_maximum_fusion.2) | copy-start | bytes 4915204
  117.7 41.7 %all-to-all-start.2 = ((f32[8,400,128]{2,1,0:T(8,128)}), f32[8,400,128]{2,1,0:T(8,128)S(1)}, u32[]{:S(2)}, u32[]{:S(2)}) async-start(f32[8,400,128]{2,1,0:T(8,128)} %collective-permute-done.3), calls=%async_computation.2 | async-start | bytes 3276800 | tf_op jit(solution)/shard_map/all_to_all | solution.py:105
  123.2 35.0 %collective-permute-start.2 = (f32[8,400,128]{2,1,0:T(8,128)S(1)}, f32[8,400,128]{2,1,0:T(8,128)}, u32[]{:S(2)}, u32[]{:S(2)}) collective-permute-start(f32[8,400,128]{2,1,0:T(8,128)S(1)} %copy-done.6), channel_id=1, source_target_pairs={{0,2},{1,3},{2,0},{3,1},{4,6},{5,7},{6,4},{7,5},{8,10},{9,11},{10,... | collective-permute-start | bytes 4915208 | tf_op jit(solution)/shard_map/ppermute | solution.py:12
  159.4 53.1 %all-to-all-start = ((f32[8,400,128]{2,1,0:T(8,128)}), f32[8,400,128]{2,1,0:T(8,128)S(1)}, u32[]{:S(2)}, u32[]{:S(2)}) async-start(f32[8,400,128]{2,1,0:T(8,128)} %collective-permute-done.2), calls=%async_computation | async-start | bytes 3276800 | tf_op jit(solution)/shard_map/all_to_all | solution.py:105
  172.4 5.8 %copy-start.1 = (f32[2560,128]{0,1:T(8,128)S(1)}, f32[2560,128]{0,1:T(8,128)}, u32[]{:S(2)}) copy-start(f32[2560,128]{0,1:T(8,128)} %copy.114) | copy-start | bytes 3932164
  212.5 6.0 %copy-start = (f32[8,400,128]{2,1,0:T(8,128)}, f32[8,400,128]{2,1,0:T(8,128)S(1)}, u32[]{:S(2)}) copy-start(f32[8,400,128]{2,1,0:T(8,128)S(1)} %all-to-all-done) | copy-start | bytes 4915204
  212.5 47.7 %all-to-all-start.3 = ((f32[8,400,128]{2,1,0:T(8,128)}), f32[8,400,128]{2,1,0:T(8,128)S(1)}, u32[]{:S(2)}, u32[]{:S(2)}) async-start(f32[8,400,128]{2,1,0:T(8,128)} %pad_maximum_fusion.5), calls=%async_computation.3 | async-start | bytes 3276800 | tf_op jit(solution)/shard_map/all_to_all | solution.py:105
  219.6 1.8 slice-start
  260.1 42.6 %all-to-all-start.4 = ((f32[8,400,128]{2,1,0:T(8,128)}), f32[8,400,128]{2,1,0:T(8,128)S(1)}, u32[]{:S(2)}, u32[]{:S(2)}) async-start(f32[8,400,128]{2,1,0:T(8,128)} %pad_maximum_fusion.7), calls=%async_computation.4 | async-start | bytes 3276800 | tf_op jit(solution)/shard_map/all_to_all | solution.py:105
  311.7 1.9 copy-start.5
  311.8 1.8 copy-start.7
  311.8 1.9 copy-start.9
